TPU v7x, 256 devices: a whole 4x4x8 slice. The times are simulated.
256 devices in a mesh: gx: 32 (over z, x), gy: 8 (over y, core).
Axes of the slice: x: 4, y: 4, z: 8, core: 2. Of those that a mesh axis runs over, the one named last changes fastest.
Arguments:
- occupied: bfloat16 [32, 128, 128, 256], P(None, 'gx', 'gy'), as said below
- search_dirs: bfloat16 [32, 128, 128, 256], P(None, 'gx', 'gy'), as said below
- previous_dirs: bfloat16 [32, 128, 128, 256], P(None, 'gx', 'gy'), as said below
- occupied_image: bfloat16 [32, 128, 128, 256], P(None, 'gx', 'gy'), as said below
- previous_image: bfloat16 [32, 128, 128, 256], P(None, 'gx', 'gy'), as said below
- potential: float32 [128, 128, 256], P('gx', 'gy'), may hold values from -18 to 0, as said below
- ritz_vectors: bfloat16 [96, 32], replicated, may hold values from -3 to 3, as said below
Outputs:
- new_block: bfloat16 [32, 128, 128, 256], P(None, 'gx', 'gy')
- ritz_matrix: float32 [32, 32], replicated
- search_image: bfloat16 [32, 128, 128, 256], P(None, 'gx', 'gy')
Inputs may be any that keep to these rules, and one draw needn't show every extreme that they name: `occupied`: orbital fields of order 1 / sqrt(4194304) a cell. `search_dirs`: orbital fields of order 1 / sqrt(4194304) a cell. `previous_dirs`: orbital fields of order 1 / sqrt(4194304) a cell. `occupied_image`: fields of order a few / sqrt(4194304) a cell. `previous_image`: fields of order a few / sqrt(4194304) a cell. `potential`: non-positive. `ritz_vectors`: the correlation of the new block is positive definite.
All inputs are finite; a program needn't handle non-finite values.
Results may differ from a plain program's by a relative error of at most 0.002.
Values may be sent and summed in bfloat16 or wider, within the bound.
A program may use at most 128 MiB of HBM per device.

v0:
```python
import jax
import jax.numpy as jnp
from jax import lax
from jax.sharding import PartitionSpec as P

COEFFS = (-205.0 / 72.0, 8.0 / 5.0, -1.0 / 5.0, 8.0 / 315.0, -1.0 / 560.0)


def extended(cells, sides, width):
    for axis, dim in sides:
        count = lax.axis_size(axis)
        head = lax.slice_in_dim(cells, 0, width, axis=dim)
        tail = lax.slice_in_dim(cells, cells.shape[dim] - width, cells.shape[dim], axis=dim)
        cells = jnp.concatenate(
            [
                lax.ppermute(tail, axis, [(i, (i + 1) % count) for i in range(count)]),
                cells,
                lax.ppermute(head, axis, [((i + 1) % count, i) for i in range(count)]),
            ],
            axis=dim,
        )
    return cells


def cropped(padded, margins, dimension, offset):
    result = padded
    for position in (1, 2):
        margin = margins[position - 1]
        length = padded.shape[position] - 2 * margin
        start = margin + (offset if position == dimension else 0)
        result = lax.slice_in_dim(result, start, start + length, axis=position)
    return result


def laplacian(padded, margins):
    center = cropped(padded, margins, 0, 0).astype(jnp.float32)
    summed = 3.0 * COEFFS[0] * center
    for dimension in (1, 2, 3):
        for offset in range(1, 5):
            if dimension < 3 and margins[dimension - 1] > 0:
                paired = cropped(padded, margins, dimension, offset).astype(jnp.float32)
                paired = paired + cropped(padded, margins, dimension, -offset).astype(jnp.float32)
            else:
                paired = jnp.roll(center, offset, dimension) + jnp.roll(center, -offset, dimension)
            summed = summed + COEFFS[offset] * paired
    return summed


def flatten(values):
    return values.reshape(values.shape[0], -1)


def contract(left_rows, right_rows):
    return lax.dot_general(
        left_rows,
        right_rows,
        (((1,), (1,)), ((), ())),
        precision=None,
        preferred_element_type=jnp.float32,
    )


def rotate(coeffs, rows):
    return lax.dot_general(
        coeffs, rows, (((0,), (0,)), ((), ())), preferred_element_type=jnp.float32
    )


def per_device(
    occupied, search_dirs, previous_dirs, occupied_image, previous_image, potential, ritz_vectors
):
    highest = lax.Precision.HIGHEST
    padded = extended(search_dirs, (("gx", 1), ("gy", 2)), 4)
    curvature = laplacian(padded, (4, 4))
    search_image = (-0.5 * curvature + potential * search_dirs.astype(jnp.float32)).astype(
        jnp.bfloat16
    )
    basis = jnp.concatenate([flatten(occupied), flatten(search_dirs), flatten(previous_dirs)], 0)
    images = jnp.concatenate(
        [flatten(occupied_image), flatten(search_image), flatten(previous_image)], 0
    )
    rotated = rotate(ritz_vectors, basis)
    gram_correlation = contract(basis, basis)
    gram_energy = contract(basis, images)
    gram_correlation, gram_energy = lax.psum((gram_correlation, gram_energy), ("gx", "gy"))
    coeff_float = ritz_vectors.astype(jnp.float32)
    proj_correlation = jnp.dot(
        coeff_float.T, jnp.dot(gram_correlation, coeff_float, precision=highest), precision=highest
    )
    proj_energy = jnp.dot(
        coeff_float.T, jnp.dot(gram_energy, coeff_float, precision=highest), precision=highest
    )
    factor = jnp.linalg.cholesky(proj_correlation)
    half_solved = lax.linalg.triangular_solve(factor, proj_energy, left_side=True, lower=True)
    ritz_matrix = lax.linalg.triangular_solve(factor, half_solved.T, left_side=True, lower=True).T
    new_block = lax.linalg.triangular_solve(factor, rotated, left_side=True, lower=True)
    new_block = new_block.astype(jnp.bfloat16).reshape(occupied.shape)
    return (new_block, ritz_matrix, search_image)


def solution(mesh):
    return jax.shard_map(
        per_device,
        mesh=mesh,
        in_specs=(
            P(None, "gx", "gy", None),
            P(None, "gx", "gy", None),
            P(None, "gx", "gy", None),
            P(None, "gx", "gy", None),
            P(None, "gx", "gy", None),
            P("gx", "gy", None),
            P(),
        ),
        out_specs=(P(None, "gx", "gy", None), P(), P(None, "gx", "gy", None)),
        check_vma=False,
    )
```

profile of v0, /device:TPU:1, one launch (start us, length us, event | category | flops | bytes accessed | tf_op | source)
XLA Modules:
  0.0 336.4 jit_solution(16917745228443968397)
XLA Ops:
  7.2 1.9 copy.22
  9.1 2.1 collective-permute-start.1
  11.2 6.6 %collective-permute-start = (bf16[32,4,16,256]{3,0,2,1:T(8,128)(2,1)S(1)}, bf16[32,4,16,256]{3,0,2,1:T(8,128)(2,1)S(1)}, u32[]{:S(2)}, u32[]{:S(2)}) collective-permute-start(bf16[32,4,16,256]{3,0,2,1:T(8,128)(2,1)S(1)} %copy.22), channel_id=1, source_target_pairs={{8,0},{16,8},{24,16},{32,24},{40,32},{48,40},{56,48},{64,56},{72,6... | collective-permute-start | bytes 3145736 | tf_op jit(solution)/shard_map/ppermute | solution.py:18
  20.6 1.0 copy-done.9
  21.6 1.6 copy.35
  23.2 1.6 copy.37
  24.8 1.6 fusion.38
  26.4 14.3 %collective-permute-done.1 = bf16[32,4,16,256]{3,0,2,1:T(8,128)(2,1)S(1)} collective-permute-done((bf16[32,4,16,256]{3,0,2,1:T(8,128)(2,1)S(1)}, bf16[32,4,16,256]{3,0,2,1:T(8,128)(2,1)S(1)}, u32[]{:S(2)}, u32[]{:S(2)}) %collective-permute-start.1) | collective-permute-done | bytes 1048608 | tf_op jit(solution)/shard_map/ppermute | solution.py:16
  41.8 1.8 fusion.31
  43.6 1.7 fusion.33
  45.3 1.7 fusion.35
  49.6 1.2 collective-permute-start.2
  50.8 1.2 collective-permute-start.3
  52.0 1.7 fusion.37
  55.2 6.8 %collective-permute-done.2 = bf16[32,12,4,256]{3,0,2,1:T(8,128)(2,1)S(1)} collective-permute-done((bf16[32,12,4,256]{3,0,2,1:T(8,128)(2,1)S(1)}, bf16[32,12,4,256]{3,0,2,1:T(8,128)(2,1)S(1)}, u32[]{:S(2)}, u32[]{:S(2)}) %collective-permute-start.2) | collective-permute-done | bytes 786464 | tf_op jit(solution)/shard_map/ppermute | solution.py:18
  63.1 11.4 %fusion.13 = bf16[32,4,16,256]{3,0,2,1:T(8,128)(2,1)S(1)} fusion(f32[32,4,16,255]{3,0,2,1:T(8,128)S(1)} %get-tuple-element.30, f32[32,4,16,1]{3,0,2,1:T(8,128)} %get-tuple-element.32, f32[32,4,16,1]{3,0,2,1:T(8,128)} %get-tuple-element.31, f32[32,4,16,255]{3,0,2,1:T(8,128)S(1)} %get-tuple-element.29, f32[32,4,16,254]{3,0,2,1:T(8,128)S(1)} %get-tuple-element.26, ...), kind=kLoop, calls=%fused_computation.27 | loop fusion | flops 38797312 | bytes 32047104 | tf_op jit(solution)/shard_map/convert_element_type | solution.py:75
  76.4 1.6 fusion
  78.0 1.9 fusion.42
  79.9 1.6 copy.28
  81.5 234.8 %all-reduce.3.cloned.1.call-done = (f32[96,96]{1,0:T(8,128)}, f32[96,96]{1,0:T(8,128)}) async-done(((f32[96,96]{1,0:T(8,128)}, f32[96,96]{1,0:T(8,128)}), (f32[96,96]{1,0:T(8,128)}, f32[96,96]{1,0:T(8,128)})) %all-reduce.3.cloned.1.call-update) | async-done | bytes 73744 | tf_op jit(solution)/shard_map/psum | solution.py:85
  317.4 2.9 cholesky.16
  321.7 2.4 custom-call.9
  326.4 1.9 convolution_convert_fusion
  328.3 1.2 copy.34
  (62 shorter events, 15.6 us)
Async XLA Ops:
  7.2 70.8 %copy-start = (bf16[96,32]{0,1:T(8,128)(2,1)S(1)}, bf16[96,32]{0,1:T(8,128)(2,1)}, u32[]{:S(2)}) copy-start(bf16[96,32]{0,1:T(8,128)(2,1)} %param.15) | copy-start | bytes 18436
  7.2 10.7 %copy-start.7 = (bf16[32,4,16,256]{3,2,1,0:T(8,128)(2,1)S(1)}, bf16[32,4,16,256]{3,2,1,0:T(8,128)(2,1)}, u32[]{:S(2)}) copy-start(bf16[32,4,16,256]{3,2,1,0:T(8,128)(2,1)} %param.9) | copy-start | bytes 3145732
  7.2 309.0 %all-reduce.3.cloned.1.call-start = ((), (), s32[]{:S(2)}) async-start(), calls=%async_computation | async-start | bytes 196608 | tf_op jit(solution)/shard_map/psum | solution.py:85
  9.1 31.6 %collective-permute-start.1 = (bf16[32,4,16,256]{3,0,2,1:T(8,128)(2,1)S(1)}, bf16[32,4,16,256]{3,0,2,1:T(8,128)(2,1)S(1)}, u32[]{:S(2)}, u32[]{:S(2)}) collective-permute-start(bf16[32,4,16,256]{3,0,2,1:T(8,128)(2,1)S(1)} %copy.22), channel_id=1, source_target_pairs={{0,8},{8,16},{16,24},{24,32},{32,40},{40,48},{48,56},{56,64},{64,7... | collective-permute-start | bytes 3145736 | tf_op jit(solution)/shard_map/ppermute | solution.py:16
  11.2 37.3 %collective-permute-start = (bf16[32,4,16,256]{3,0,2,1:T(8,128)(2,1)S(1)}, bf16[32,4,16,256]{3,0,2,1:T(8,128)(2,1)S(1)}, u32[]{:S(2)}, u32[]{:S(2)}) collective-permute-start(bf16[32,4,16,256]{3,0,2,1:T(8,128)(2,1)S(1)} %copy.22), channel_id=1, source_target_pairs={{8,0},{16,8},{24,16},{32,24},{40,32},{48,40},{56,48},{64,56},{72,6... | collective-permute-start | bytes 3145736 | tf_op jit(solution)/shard_map/ppermute | solution.py:18
  17.9 1.2 copy-start.1
  18.5 1.3 copy-start.8
  20.4 1.2 copy-start.9
  20.5 2.7 copy-start.10
  40.7 1.1 copy-start.5
  48.5 1.1 copy-start.6
  49.6 12.4 %collective-permute-start.2 = (bf16[32,12,4,256]{3,0,2,1:T(8,128)(2,1)S(1)}, bf16[32,12,4,256]{3,0,2,1:T(8,128)(2,1)S(1)}, u32[]{:S(2)}, u32[]{:S(2)}) collective-permute-start(bf16[32,12,4,256]{3,0,2,1:T(8,128)(2,1)S(1)} %get-tuple-element.15), channel_id=1, source_target_pairs={{1,0},{2,1},{3,2},{4,3},{5,4},{6,5},{7,6},{0,7},{9,8},{10,9},{11,1... | collective-permute-start | bytes 2359304 | tf_op jit(solution)/shard_map/ppermute | solution.py:18
  50.8 11.2 %collective-permute-start.3 = (bf16[32,12,4,256]{3,0,2,1:T(8,128)(2,1)S(1)}, bf16[32,12,4,256]{3,0,2,1:T(8,128)(2,1)S(1)}, u32[]{:S(2)}, u32[]{:S(2)}) collective-permute-start(bf16[32,12,4,256]{3,0,2,1:T(8,128)(2,1)S(1)} %get-tuple-element.16), channel_id=1, source_target_pairs={{0,1},{1,2},{2,3},{3,4},{4,5},{5,6},{6,7},{7,0},{8,9},{9,10},{10,1... | collective-permute-start | bytes 2359304 | tf_op jit(solution)/shard_map/ppermute | solution.py:16
  54.4 8.7 %copy-start.15 = (f32[4,16,256]{2,1,0:T(8,128)S(1)}, f32[4,16,256]{2,1,0:T(8,128)}, u32[]{:S(2)}) copy-start(f32[4,16,256]{2,1,0:T(8,128)} %param.14) | copy-start | bytes 196612
  61.9 0.9 copy-start.13
  61.9 1.1 copy-start.14
  74.5 1.0 copy-start.2
  74.5 1.6 copy-start.11
  74.5 1.9 copy-start.12
  78.0 1.9 copy-start.3
  79.9 246.5 %copy-start.4 = (f32[16384,32]{0,1:T(8,128)S(1)}, f32[16384,32]{0,1:T(8,128)}, u32[]{:S(2)}) copy-start(f32[16384,32]{0,1:T(8,128)} %fusion.42) | copy-start | bytes 6291460
Sparse Core Ops, SparseCore 0:
  78.1 238.0 all-reduce.2
where the time goes:
time: 337 us; the launch traced here: 336 us
  waiting for transfers between devices  256 us (76%)
  local copies, waits for them, and re-layouts  26.5 us (8%)
  other arithmetic  18.9 us (6%)
  between operations  14.3 us (4%)
  starting transfers between devices  11.2 us (3%)
  matrix products  9.63 us (3%)
    psum x1, waiting for transfers between devices, per_device(): lax.psum((gram_correlation, gram_energy), ('gx', 'gy'))  235 us
    unnamed x44, local copies, waits for them, and re-layouts  14.4 us
    ppermute x2, waiting for transfers between devices, extended(): lax.ppermute(tail, axis, [(i, (i + 1) % count) for i in range(count)])  14.3 us
    convert_element_type x1, other arithmetic, per_device(): (-0.5 * curvature + potential * search_dirs.astype(jnp.float32)).astype(j...  11.4 us
    slice x8, local copies, waits for them, and re-layouts, laplacian(): jnp.roll(center, -offset, dimension)  9.81 us
    ppermute x2, starting transfers between devices, extended(): lax.ppermute(head, axis, [((i + 1) % count, i) for i in range(count)])  7.88 us
    ppermute x2, waiting for transfers between devices, extended(): lax.ppermute(head, axis, [((i + 1) % count, i) for i in range(count)])  6.78 us
  transfers between devices with their start and end apart: 5, of which 3 were waited for; matrix products, arithmetic and copies ran while one was open for 6% of the time, Pallas kernels for 0%

commit v1 on v0

v1 whole, which is shorter than its diff:
```python
import itertools

import jax
import jax.numpy as jnp
import ml_dtypes
import numpy as np
from jax import lax
from jax.experimental import pallas as pl
from jax.experimental.pallas import tpu as pltpu
from jax.sharding import PartitionSpec as P

MESH = pl.DeviceIdType.MESH
HIGHEST = lax.Precision.HIGHEST
F32, BF16 = jnp.float32, jnp.bfloat16

ORB = 32
LX, LY, LZ = 4, 16, 256
NGX, NGY = 32, 8
NXC, NYC, NZC, NC = 4, 4, 8, 2
CH = 4
NCH = ORB // CH
GR = 16
ROWS = ORB * LY

SCALE = 5040.0
SIDE = {1: 8064.0, 2: -1008.0, 3: 128.0, 4: -9.0}
CENTRE = 0.5 * 3.0 * 205.0 / 72.0


def side(distance):
    return SIDE.get(abs(distance), 0.0)


def stencil_matrices():
    own, xl, xr, yl, yr = (np.zeros((LX, LY, LX, LY)) for _ in range(5))
    for x, y, u, v in itertools.product(range(LX), range(LY), range(LX), range(LY)):
        if y == v:
            own[x, y, u, v] += side(x - u)
            xl[x, y, u, v] = side(x - (u - LX))
            xr[x, y, u, v] = side(x - (u + LX))
        if x == u:
            own[x, y, u, v] += side(y - v)
            yl[x, y, u, v] = side(y - (v - LY))
            yr[x, y, u, v] = side(y - (v + LY))
    n = LX * LY
    blocks = [np.kron(np.eye(CH), part.reshape(n, n)) for part in (own, xl, xr, yl, yr)]
    along = np.zeros((LZ, LZ))
    for z in range(LZ):
        for d in (1, 2, 3, 4):
            along[z, (z + d) % LZ] += SIDE[d]
            along[z, (z - d) % LZ] += SIDE[d]
    return np.concatenate(blocks, 1).astype(ml_dtypes.bfloat16), along.astype(ml_dtypes.bfloat16)


def dot(a, b, precision=None):
    return jnp.dot(a, b, preferred_element_type=F32, precision=precision)


def dot_nt(a, b, precision=None):
    return lax.dot_general(a, b, (((1,), (1,)), ((), ())), preferred_element_type=F32, precision=precision)


def ring_distance(d, n):
    return min(d, n - d)


XY_OFFSETS = sorted(
    [o for o in itertools.product(range(NXC), range(NYC)) if o != (0, 0)],
    key=lambda o: -(ring_distance(o[0], NXC) + ring_distance(o[1], NYC)),
)
ZC_OFFSETS = sorted(
    [o for o in itertools.product(range(NZC), range(NC)) if o != (0, 0)],
    key=lambda o: -(ring_distance(o[0], NZC) + 0.5 * o[1]),
)


def kernel(
    occ, sea, pre, occ_im, pre_im, pot, ritz, amat, zmat, rep, rep96,
    nb_out, ritz_out, si_out,
    o_v, s_v, p_v, oi_v, pi_v, v_v, xl, xr, yl, yr, si_v, nb_v, rk, rot, grams, rr, kh, kl,
    c1, c2, e1, e2,
    load_sem, send_sem, recv_sem, out_sem, c1s, c1r, c2s, c2r, e1s, e1r, e2s, e2r,
):
    gx, gy = lax.axis_index("gx"), lax.axis_index("gy")
    z, x, y, core = gx // NXC, lax.rem(gx, NXC), gy // NC, lax.rem(gy, NC)
    xp, xm = lax.rem(gx + 1, NGX), lax.rem(gx + NGX - 1, NGX)
    yp, ym = lax.rem(gy + 1, NGY), lax.rem(gy + NGY - 1, NGY)
    neighbours = [(xp, gy), (xm, gy), (gx, yp), (gx, ym)]

    loads = [
        pltpu.make_async_copy(src, dst, load_sem.at[i])
        for i, (src, dst) in enumerate(
            ((occ, o_v), (sea, s_v), (pre, p_v), (occ_im, oi_v), (pre_im, pi_v), (pot, v_v))
        )
    ]
    for load in loads:
        load.start()

    xy_group = []
    for dx, dy in XY_OFFSETS:
        px, py = lax.rem(x + dx, NXC), lax.rem(y + dy, NYC)
        xy_group.append((px * NYC + py, (z * NXC + px, py * NC + core)))
    zc_group = []
    for dz, dc in ZC_OFFSETS:
        pz, pc = lax.rem(z + dz, NZC), lax.rem(core + dc, NC)
        zc_group.append((pz * NC + pc, (pz * NXC + x, y * NC + pc)))
    xy_me, zc_me = x * NYC + y, z * NC + core

    barrier = pltpu.get_barrier_semaphore()
    others = neighbours + [d for _, d in xy_group] + [d for _, d in zc_group]
    for device in others:
        pl.semaphore_signal(barrier, inc=1, device_id=device, device_id_type=MESH)
    pl.semaphore_wait(barrier, len(others))

    halos = (xl, xr, yl, yr)

    def halo_copy(way, c):
        part = pl.ds(c * CH, CH)
        return pltpu.make_async_remote_copy(
            sea.at[part], halos[way].at[part], send_sem.at[way, c], recv_sem.at[way, c],
            device_id=neighbours[way], device_id_type=MESH,
        )

    for c in range(NCH):
        for way in range(4):
            halo_copy(way, c).start()

    def post(buf, me, group, sends, recvs, value):
        buf[me] = value
        for i, (_, device) in enumerate(group):
            pltpu.make_async_remote_copy(
                buf.at[me], buf.at[me], sends.at[i], recvs.at[me], device_id=device, device_id_type=MESH
            ).start()

    def collect(buf, me, group, sends, recvs):
        for i, (slot, device) in enumerate(group):
            pltpu.make_async_remote_copy(
                buf.at[slot], buf.at[slot], sends.at[i], recvs.at[slot], device_id=device, device_id_type=MESH
            ).wait_recv()
        total = buf[0]
        for slot in range(1, 16):
            total = total + buf[slot]
        return total

    def drain(buf, me, group, sends, recvs):
        for i, (_, device) in enumerate(group):
            pltpu.make_async_remote_copy(
                buf.at[me], buf.at[me], sends.at[i], recvs.at[me], device_id=device, device_id_type=MESH
            ).wait_send()

    def pack(square):
        return jnp.concatenate([square[8 * b : 8 * b + 8, :] for b in range(4)], axis=1)

    def unpack(packed):
        return jnp.concatenate([packed[:, 32 * b : 32 * b + 32] for b in range(4)], axis=0)

    def same_y(width):
        row = lax.broadcasted_iota(jnp.int32, (LY, width), 0)
        column = lax.broadcasted_iota(jnp.int32, (LY, width), 1)
        return jnp.where(row == (column & (LY - 1)), 1.0, 0.0).astype(F32)

    def masked(values):
        width = values.shape[1]
        return values.reshape(-1, LY, width) * same_y(width)[None]

    ritz_cols = dot(ritz[...].astype(F32).T.astype(BF16), rep96[...].T).astype(BF16)
    for block in range(3):
        spread = dot(rep[...], ritz_cols[:, block * ROWS : (block + 1) * ROWS])
        rk[:, block * ROWS : (block + 1) * ROWS] = masked(spread).reshape(ROWS, ROWS).astype(BF16)

    loads[0].wait()
    loads[1].wait()
    loads[2].wait()

    @pl.loop(0, LX)
    def _(i):
        rows = jnp.concatenate([ref[:, i].reshape(ROWS, LZ) for ref in (o_v, s_v, p_v)], axis=0)
        rotated = dot(rk[...], rows)
        high = rotated.astype(BF16)
        columns = pl.ds(pl.multiple_of(i * LZ, LZ), LZ)
        rot[0:ROWS, columns] = high
        rot[ROWS : 2 * ROWS, columns] = (rotated - high.astype(F32)).astype(BF16)

    products = dot_nt(rot[0:ROWS, :], rot[...])
    folded = masked(products).sum(axis=1)
    high_high = dot(folded[:, 0:ROWS], rep[...].astype(F32), HIGHEST)
    high_low = dot(folded[:, ROWS : 2 * ROWS], rep[...].astype(F32), HIGHEST)
    correlation = high_high + high_low + high_low.T
    post(c1, xy_me, xy_group, c1s, c1r, pack(correlation))

    def gram(ref, first):
        rows = jnp.concatenate([ref[first : first + GR, i].reshape(GR * LY, LZ) for i in range(LX)], axis=1)
        products = dot_nt(rot[...], rows)
        return masked(products[0:ROWS] + products[ROWS : 2 * ROWS]).sum(axis=1)

    loads[3].wait()
    grams[:, 0:256] = gram(oi_v, 0)
    grams[:, 256:512] = gram(oi_v, GR)
    post(c2, zc_me, zc_group, c2s, c2r, collect(c1, xy_me, xy_group, c1s, c1r))
    loads[4].wait()
    grams[:, 1024:1280] = gram(pi_v, 0)
    grams[:, 1280:1536] = gram(pi_v, GR)
    correlation = unpack(collect(c2, zc_me, zc_group, c2s, c2r))

    lane = lax.broadcasted_iota(jnp.int32, (ORB, 2 * ORB), 1)
    row = lax.broadcasted_iota(jnp.int32, (ORB, 2 * ORB), 0)
    identity = jnp.where(lane == row + ORB, 1.0, 0.0).astype(F32)
    work = jnp.concatenate([correlation, identity[:, ORB:]], axis=1)
    row_number = lax.broadcasted_iota(jnp.int32, (ORB, 1), 0)
    for k in range(ORB):
        pivot_row = work[k : k + 1, :]
        scaled = pivot_row / work[k : k + 1, k : k + 1]
        column = jnp.where(row_number > k, work[:, k : k + 1], 0.0)
        work = work - column * scaled
    pivots = jnp.sum(jnp.where(lane == row, work, 0.0), axis=1, keepdims=True)
    inverse = work[:, ORB : 2 * ORB] / jnp.sqrt(pivots)

    inverse_high = inverse.astype(BF16)
    inverse_low = (inverse - inverse_high.astype(F32)).astype(BF16)
    for ref, part in ((kh, inverse_high), (kl, inverse_low)):
        spread = dot(rep[...], dot_nt(part, rep[...]).astype(BF16))
        ref[...] = masked(spread).reshape(ROWS, ROWS).astype(BF16)

    @pl.loop(0, LX)
    def _(i):
        columns = pl.ds(pl.multiple_of(i * LZ, LZ), LZ)
        high, low = rot[0:ROWS, columns], rot[ROWS : 2 * ROWS, columns]
        block = dot(kh[...], high) + (dot(kl[...], high) + dot(kh[...], low))
        nb_v[:, i] = block.astype(BF16).reshape(ORB, LY, LZ)

    nb_store = pltpu.make_async_copy(nb_v, nb_out, out_sem.at[NCH])
    nb_store.start()

    ritz_spread = dot(rep96[...], ritz[...])
    rr[...] = dot_nt(ritz_spread, inverse, HIGHEST)

    loads[5].wait()

    def stencil_chunk(c):
        for way in range(4):
            halo_copy(way, c).wait_recv()
        part = pl.ds(c * CH, CH)
        n = CH * LX * LY
        own = s_v[part].reshape(n, LZ)
        rows = jnp.concatenate([own] + [ref[part].reshape(n, LZ) for ref in halos], axis=0)
        summed = dot(amat[...], rows) + dot(own, zmat[...])
        weight = (v_v[...] + CENTRE).reshape(1, LX * LY, LZ)
        image = weight * own.astype(F32).reshape(CH, LX * LY, LZ)
        image = image - (0.5 / SCALE) * summed.reshape(CH, LX * LY, LZ)
        si_v[part] = image.astype(BF16).reshape(CH, LX, LY, LZ)
        pltpu.make_async_copy(si_v.at[part], si_out.at[part], out_sem.at[c]).start()

    @pl.loop(0, NCH // 2)
    def _(c):
        stencil_chunk(c)

    grams[:, 512:768] = gram(si_v, 0)
    early = dot(grams[:, 0:768], rr[0:768, :], HIGHEST) + dot(grams[:, 1024:1536], rr[1024:1536, :], HIGHEST)

    @pl.loop(NCH // 2, NCH)
    def _(c):
        stencil_chunk(c)

    energy = early + dot(gram(si_v, GR), rr[768:1024, :], HIGHEST)
    energy = dot(inverse, energy, HIGHEST)
    post(e1, xy_me, xy_group, e1s, e1r, pack(energy))
    post(e2, zc_me, zc_group, e2s, e2r, collect(e1, xy_me, xy_group, e1s, e1r))

    for way in range(4):
        for c in range(NCH):
            halo_copy(way, c).wait_send()
    for c in range(NCH):
        part = pl.ds(c * CH, CH)
        pltpu.make_async_copy(si_v.at[part], si_out.at[part], out_sem.at[c]).wait()
    nb_store.wait()
    drain(c1, xy_me, xy_group, c1s, c1r)
    drain(c2, zc_me, zc_group, c2s, c2r)
    drain(e1, xy_me, xy_group, e1s, e1r)
    ritz_out[...] = unpack(collect(e2, zc_me, zc_group, e2s, e2r))
    drain(e2, zc_me, zc_group, e2s, e2r)


def per_device(occupied, search_dirs, previous_dirs, occupied_image, previous_image, potential, ritz_vectors):
    amat, zmat = stencil_matrices()
    rep96 = np.kron(np.eye(3 * ORB), np.ones((LY, 1))).astype(ml_dtypes.bfloat16)
    rep = np.kron(np.eye(ORB), np.ones((LY, 1))).astype(ml_dtypes.bfloat16)
    anywhere = pl.BlockSpec(memory_space=pl.ANY)
    vmem = pl.BlockSpec(memory_space=pltpu.VMEM)
    block = (ORB, LX, LY, LZ)
    dma = pltpu.SemaphoreType.DMA
    return pl.pallas_call(
        kernel,
        out_shape=(
            jax.ShapeDtypeStruct(block, BF16),
            jax.ShapeDtypeStruct((ORB, ORB), F32),
            jax.ShapeDtypeStruct(block, BF16),
        ),
        in_specs=[anywhere] * 6 + [vmem] * 5,
        out_specs=(anywhere, vmem, anywhere),
        scratch_shapes=[pltpu.VMEM(block, BF16)] * 5
        + [pltpu.VMEM((LX, LY, LZ), F32)]
        + [pltpu.VMEM(block, BF16)] * 6
        + [
            pltpu.VMEM((ROWS, 3 * ROWS), BF16),
            pltpu.VMEM((2 * ROWS, LX * LZ), BF16),
            pltpu.VMEM((ORB, 3 * ROWS), F32),
            pltpu.VMEM((3 * ROWS, ORB), F32),
            pltpu.VMEM((ROWS, ROWS), BF16),
            pltpu.VMEM((ROWS, ROWS), BF16),
        ]
        + [pltpu.VMEM((16, 8, 128), F32)] * 4
        + [dma((6,)), dma((4, NCH)), dma((4, NCH)), dma((NCH + 1,))]
        + [dma((16,))] * 8,
        compiler_params=pltpu.CompilerParams(
            collective_id=0, has_side_effects=True, vmem_limit_bytes=56 * 2**20
        ),
    )(
        occupied, search_dirs, previous_dirs, occupied_image, previous_image, potential, ritz_vectors,
        jnp.asarray(amat), jnp.asarray(zmat), jnp.asarray(rep), jnp.asarray(rep96),
    )


def solution(mesh):
    cells = P(None, "gx", "gy", None)
    return jax.shard_map(
        per_device,
        mesh=mesh,
        in_specs=(cells, cells, cells, cells, cells, P("gx", "gy", None), P()),
        out_specs=(cells, P(), cells),
        check_vma=False,
    )
```

time: 337 us -> 73.7 us (0.22)
  waiting for transfers between devices: 256 us -> 0 us
  Pallas kernels: 0 us -> 67.5 us
  local copies, waits for them, and re-layouts: 26.5 us -> 5.38 us
  other arithmetic: 18.9 us -> 0 us
  between operations: 14.3 us -> 0.66 us
  starting transfers between devices: 11.2 us -> 0 us
  matrix products: 9.63 us -> 0 us
    psum x1 -> x0, waiting for transfers between devices: 235 us -> none  [per_device(): lax.psum((gram_correlation, gram_energy), ('gx', 'gy'))]
    pallas_call x0 -> x1, Pallas kernels: none -> 67.5 us  [per_device(): pl.pallas_call(kernel, out_shape=(jax.ShapeDtypeStruct(block, BF16), jax....]
    ppermute x4 -> x0, waiting for transfers between devices: 21.1 us -> none  [the longest x2 14.3 us: extended(): lax.ppermute(tail, axis, [(i, (i + 1) % count) for i in range(count)])]
    convert_element_type x1 -> x0, other arithmetic: 11.4 us -> none  [per_device(): (-0.5 * curvature + potential * search_dirs.astype(jnp.float32)).astype(j...]
    ppermute x4 -> x0, starting transfers between devices: 11.2 us -> none  [the longest x2 7.88 us: extended(): lax.ppermute(head, axis, [((i + 1) % count, i) for i in range(count)])]
    slice x9 -> x0, local copies, waits for them, and re-layouts: 10 us -> none  [the longest x8 9.81 us: laplacian(): jnp.roll(center, -offset, dimension)]
    unnamed x44 -> x8, local copies, waits for them, and re-layouts: 14.4 us -> 5.38 us
    dot_general x7 -> x0, matrix products: 7.3 us -> none  [the longest x2 3.18 us: contract(): lax.dot_general(left_rows, right_rows, (((1,), (1,)), ((), ())), precisio...]
  transfers between devices with their start and end apart: 5 -> 0, of which waited for: 3 -> 0; matrix products, arithmetic and copies ran while one was open for 6% -> 0% of each run, Pallas kernels for 0% -> 0%
where the time goes in v1:
time: 73.7 us; the launch traced here: 73.5 us
  Pallas kernels  67.5 us (92%)
  local copies, waits for them, and re-layouts  5.38 us (7%)
    pallas_call x1, Pallas kernels, per_device(): pl.pallas_call(kernel, out_shape=(jax.ShapeDtypeStruct(block, BF16), jax....  67.5 us
    unnamed x8, local copies, waits for them, and re-layouts  5.38 us

profile of v1, /device:TPU:1, one launch (start us, length us, event | category | flops | bytes accessed | tf_op | source)
XLA Modules:
  0.0 73.5 jit_solution(4319104949877570044)
XLA Ops:
  0.6 1.4 %copy.14.ritz = bf16[96,32]{1,0:T(8,128)(2,1)} copy(bf16[96,32]{0,1:T(8,128)(2,1)} %param.17) | data formatting | bytes 12288 | tf_op args[6]
  2.0 67.5 %shard_map.130 = (bf16[32,4,16,256]{3,2,1,0:T(8,128)(2,1)}, f32[32,32]{1,0:T(8,128)}, bf16[32,4,16,256]{3,2,1,0:T(8,128)(2,1)}) custom-call(bf16[32,4,16,256]{3,2,1,0:T(8,128)(2,1)} %occ.1, bf16[32,4,16,256]{3,2,1,0:T(8,128)(2,1)} %sea.1, bf16[32,4,16,256]{3,2,1,0:T(8,128)(2,1)} %pre.1, bf16[32,4,16,256]{3,2,1,0:T(8,128)(2,1)} %occ_im.1, ...), custom_call_target="tpu_custom_call" | custom-call | tf_op jit(solution)/shard_map/pallas_call | solution.py:291
  69.5 0.0 copy-start.1
  69.5 0.0 copy-start
  69.6 2.4 %copy.18 = bf16[32,4,16,256]{3,2,1,0:T(8,128)(2,1)} copy(bf16[32,4,16,256]{3,2,1,0:T(8,128)(2,1)} %get-tuple-element.6) | data formatting | bytes 2097152
  71.9 0.0 copy-done.1
  72.0 0.6 copy.19
  72.6 0.0 copy-done
  72.6 1.0 %copy.20 = bf16[32,4,16,256]{3,2,1,0:T(8,128)(2,1)} copy(bf16[32,4,16,256]{3,2,1,0:T(8,128)(2,1)S(1)} %copy-done) | data formatting | bytes 2097152
Async XLA Ops:
  69.5 2.4 %copy-start.1 = (f32[32,32]{1,0:T(8,128)S(1)}, f32[32,32]{1,0:T(8,128)}, u32[]{:S(2)}) copy-start(f32[32,32]{1,0:T(8,128)} %get-tuple-element.7) | copy-start | bytes 12292
  69.5 3.0 %copy-start = (bf16[32,4,16,256]{3,2,1,0:T(8,128)(2,1)S(1)}, bf16[32,4,16,256]{3,2,1,0:T(8,128)(2,1)}, u32[]{:S(2)}) copy-start(bf16[32,4,16,256]{3,2,1,0:T(8,128)(2,1)} %get-tuple-element.8) | copy-start | bytes 3145732

commit v2 on v1

--- a/solution.py
+++ b/solution.py
@@ -17,6 +17,8 @@
 LX, LY, LZ = 4, 16, 256
 NGX, NGY = 32, 8
 NXC, NYC, NZC, NC = 4, 4, 8, 2
+SENT = (3, 6)
+EARLY = 1
 CH = 4
 NCH = ORB // CH
 GR = 16
@@ -29,6 +31,14 @@
 
 def side(distance):
     return SIDE.get(abs(distance), 0.0)
+
+
+def lane_blocks(matrix):
+    return np.concatenate(np.split(matrix, matrix.shape[1] // 128, axis=1), 0).astype(ml_dtypes.bfloat16)
+
+
+def side_by_side(ref, rows):
+    return jnp.concatenate([ref[first : first + rows] for first in range(0, ref.shape[0], rows)], axis=1)
 
 
 def stencil_matrices():
@@ -49,7 +59,7 @@
         for d in (1, 2, 3, 4):
             along[z, (z + d) % LZ] += SIDE[d]
             along[z, (z - d) % LZ] += SIDE[d]
-    return np.concatenate(blocks, 1).astype(ml_dtypes.bfloat16), along.astype(ml_dtypes.bfloat16)
+    return lane_blocks(np.concatenate(blocks, 1)), lane_blocks(along)
 
 
 def dot(a, b, precision=None):
@@ -58,6 +68,16 @@
 
 def dot_nt(a, b, precision=None):
     return lax.dot_general(a, b, (((1,), (1,)), ((), ())), preferred_element_type=F32, precision=precision)
+
+
+def dot_split(a, b):
+    first = a.astype(BF16)
+    rest = a - first.astype(F32)
+    second = rest.astype(BF16)
+    third = (rest - second.astype(F32)).astype(BF16)
+    n = a.shape[0]
+    parts = dot(jnp.concatenate([first, second, third], axis=0), b)
+    return parts[0:n] + (parts[n : 2 * n] + parts[2 * n : 3 * n])
 
 
 def ring_distance(d, n):
@@ -75,11 +95,11 @@
 
 
 def kernel(
-    occ, sea, pre, occ_im, pre_im, pot, ritz, amat, zmat, rep, rep96,
-    nb_out, ritz_out, si_out,
-    o_v, s_v, p_v, oi_v, pi_v, v_v, xl, xr, yl, yr, si_v, nb_v, rk, rot, grams, rr, kh, kl,
+    occ, sea, pre, occ_im, pre_im, pot, ritz_in, amat_in, zmat_in, rep_in, rep96_in,
+    nb_v, ritz_out, si_v,
+    o_v, s_v, p_v, oi_v, pi_v, v_v, xl, xr, yl, yr, rk, rot, grams, kh, kl, ritz, amat, zmat, rep, rep96,
     c1, c2, e1, e2,
-    load_sem, send_sem, recv_sem, out_sem, c1s, c1r, c2s, c2r, e1s, e1r, e2s, e2r,
+    load_sem, send_sem, recv_sem, c1s, c1r, c2s, c2r, e1s, e1r, e2s, e2r,
 ):
     gx, gy = lax.axis_index("gx"), lax.axis_index("gy")
     z, x, y, core = gx // NXC, lax.rem(gx, NXC), gy // NC, lax.rem(gy, NC)
@@ -90,11 +110,12 @@
     loads = [
         pltpu.make_async_copy(src, dst, load_sem.at[i])
         for i, (src, dst) in enumerate(
-            ((occ, o_v), (sea, s_v), (pre, p_v), (occ_im, oi_v), (pre_im, pi_v), (pot, v_v))
+            (
+                (ritz_in, ritz), (rep96_in, rep96), (rep_in, rep), (occ, o_v), (sea, s_v), (pre, p_v),
+                (occ_im, oi_v), (pre_im, pi_v), (pot, v_v), (amat_in, amat), (zmat_in, zmat),
+            )
         )
     ]
-    for load in loads:
-        load.start()
 
     xy_group = []
     for dx, dy in XY_OFFSETS:
@@ -121,9 +142,15 @@
             device_id=neighbours[way], device_id_type=MESH,
         )
 
-    for c in range(NCH):
-        for way in range(4):
-            halo_copy(way, c).start()
+    def send_chunks(first, last):
+        for c in range(first, last):
+            for way in range(4):
+                halo_copy(way, c).start()
+
+    send_chunks(0, 1)
+    for load in loads:
+        load.start()
+    send_chunks(1, SENT[0])
 
     def post(buf, me, group, sends, recvs, value):
         buf[me] = value
@@ -163,14 +190,17 @@
         width = values.shape[1]
         return values.reshape(-1, LY, width) * same_y(width)[None]
 
-    ritz_cols = dot(ritz[...].astype(F32).T.astype(BF16), rep96[...].T).astype(BF16)
+    for load in loads[:3]:
+        load.wait()
+
+    ritz_cols = dot_nt(ritz[...], rep96[...]).astype(BF16)
     for block in range(3):
         spread = dot(rep[...], ritz_cols[:, block * ROWS : (block + 1) * ROWS])
         rk[:, block * ROWS : (block + 1) * ROWS] = masked(spread).reshape(ROWS, ROWS).astype(BF16)
-
-    loads[0].wait()
-    loads[1].wait()
-    loads[2].wait()
+    ritz_rows = dot_nt(rep96[...], ritz[...]).astype(BF16)
+
+    for load in loads[3:6]:
+        load.wait()
 
     @pl.loop(0, LX)
     def _(i):
@@ -183,24 +213,62 @@
 
     products = dot_nt(rot[0:ROWS, :], rot[...])
     folded = masked(products).sum(axis=1)
-    high_high = dot(folded[:, 0:ROWS], rep[...].astype(F32), HIGHEST)
-    high_low = dot(folded[:, ROWS : 2 * ROWS], rep[...].astype(F32), HIGHEST)
+    high_high = dot_split(folded[:, 0:ROWS], rep[...])
+    high_low = dot_split(folded[:, ROWS : 2 * ROWS], rep[...])
     correlation = high_high + high_low + high_low.T
-    post(c1, xy_me, xy_group, c1s, c1r, pack(correlation))
+    post(c1, zc_me, zc_group, c1s, c1r, pack(correlation))
+    send_chunks(SENT[0], SENT[1])
 
     def gram(ref, first):
         rows = jnp.concatenate([ref[first : first + GR, i].reshape(GR * LY, LZ) for i in range(LX)], axis=1)
         products = dot_nt(rot[...], rows)
         return masked(products[0:ROWS] + products[ROWS : 2 * ROWS]).sum(axis=1)
 
-    loads[3].wait()
+    for load in loads[8:]:
+        load.wait()
+
+    def stencil_chunk(c):
+        for way in range(4):
+            halo_copy(way, c).wait_recv()
+        part = pl.ds(c * CH, CH)
+        n = CH * LX * LY
+        own = s_v[part].reshape(n, LZ)
+        rows = jnp.concatenate([own] + [ref[part].reshape(n, LZ) for ref in halos], axis=0)
+        summed = dot(side_by_side(amat, n), rows) + dot(own, side_by_side(zmat, LZ))
+        weight = (v_v[...] + CENTRE).reshape(1, LX * LY, LZ)
+        image = weight * own.astype(F32).reshape(CH, LX * LY, LZ)
+        image = image - (0.5 / SCALE) * summed.reshape(CH, LX * LY, LZ)
+        si_v[part] = image.astype(BF16).reshape(CH, LX, LY, LZ)
+
+    loads[6].wait()
     grams[:, 0:256] = gram(oi_v, 0)
     grams[:, 256:512] = gram(oi_v, GR)
-    post(c2, zc_me, zc_group, c2s, c2r, collect(c1, xy_me, xy_group, c1s, c1r))
-    loads[4].wait()
-    grams[:, 1024:1280] = gram(pi_v, 0)
-    grams[:, 1280:1536] = gram(pi_v, GR)
-    correlation = unpack(collect(c2, zc_me, zc_group, c2s, c2r))
+    loads[7].wait()
+    grams[:, 768:1024] = gram(pi_v, 0)
+    grams[:, 1024:1280] = gram(pi_v, GR)
+
+    @pl.loop(0, EARLY)
+    def _(c):
+        stencil_chunk(c)
+
+    post(c2, xy_me, xy_group, c2s, c2r, collect(c1, zc_me, zc_group, c1s, c1r))
+    send_chunks(SENT[1], NCH)
+
+    @pl.loop(EARLY, NCH // 2)
+    def _(c):
+        stencil_chunk(c)
+
+    grams[:, 512:768] = gram(si_v, 0)
+    early = dot_split(grams[:, 0:768], ritz_rows[0:768]) + dot_split(grams[:, 768:1280], ritz_rows[1024:1536])
+
+    @pl.loop(NCH // 2, NCH)
+    def _(c):
+        stencil_chunk(c)
+
+    energy = early + dot_split(gram(si_v, GR), ritz_rows[768:1024])
+    post(e1, xy_me, xy_group, e1s, e1r, pack(energy))
+
+    correlation = unpack(collect(c2, xy_me, xy_group, c2s, c2r))
 
     lane = lax.broadcasted_iota(jnp.int32, (ORB, 2 * ORB), 1)
     row = lax.broadcasted_iota(jnp.int32, (ORB, 2 * ORB), 0)
@@ -221,63 +289,38 @@
         spread = dot(rep[...], dot_nt(part, rep[...]).astype(BF16))
         ref[...] = masked(spread).reshape(ROWS, ROWS).astype(BF16)
 
-    @pl.loop(0, LX)
-    def _(i):
+    post(e2, zc_me, zc_group, e2s, e2r, collect(e1, xy_me, xy_group, e1s, e1r))
+
+    def rotate(i):
         columns = pl.ds(pl.multiple_of(i * LZ, LZ), LZ)
         high, low = rot[0:ROWS, columns], rot[ROWS : 2 * ROWS, columns]
         block = dot(kh[...], high) + (dot(kl[...], high) + dot(kh[...], low))
         nb_v[:, i] = block.astype(BF16).reshape(ORB, LY, LZ)
 
-    nb_store = pltpu.make_async_copy(nb_v, nb_out, out_sem.at[NCH])
-    nb_store.start()
-
-    ritz_spread = dot(rep96[...], ritz[...])
-    rr[...] = dot_nt(ritz_spread, inverse, HIGHEST)
-
-    loads[5].wait()
-
-    def stencil_chunk(c):
-        for way in range(4):
-            halo_copy(way, c).wait_recv()
-        part = pl.ds(c * CH, CH)
-        n = CH * LX * LY
-        own = s_v[part].reshape(n, LZ)
-        rows = jnp.concatenate([own] + [ref[part].reshape(n, LZ) for ref in halos], axis=0)
-        summed = dot(amat[...], rows) + dot(own, zmat[...])
-        weight = (v_v[...] + CENTRE).reshape(1, LX * LY, LZ)
-        image = weight * own.astype(F32).reshape(CH, LX * LY, LZ)
-        image = image - (0.5 / SCALE) * summed.reshape(CH, LX * LY, LZ)
-        si_v[part] = image.astype(BF16).reshape(CH, LX, LY, LZ)
-        pltpu.make_async_copy(si_v.at[part], si_out.at[part], out_sem.at[c]).start()
-
-    @pl.loop(0, NCH // 2)
-    def _(c):
-        stencil_chunk(c)
-
-    grams[:, 512:768] = gram(si_v, 0)
-    early = dot(grams[:, 0:768], rr[0:768, :], HIGHEST) + dot(grams[:, 1024:1536], rr[1024:1536, :], HIGHEST)
-
-    @pl.loop(NCH // 2, NCH)
-    def _(c):
-        stencil_chunk(c)
-
-    energy = early + dot(gram(si_v, GR), rr[768:1024, :], HIGHEST)
-    energy = dot(inverse, energy, HIGHEST)
-    post(e1, xy_me, xy_group, e1s, e1r, pack(energy))
-    post(e2, zc_me, zc_group, e2s, e2r, collect(e1, xy_me, xy_group, e1s, e1r))
+    @pl.loop(0, LX)
+    def _(i):
+        rotate(i)
 
     for way in range(4):
         for c in range(NCH):
             halo_copy(way, c).wait_send()
-    for c in range(NCH):
-        part = pl.ds(c * CH, CH)
-        pltpu.make_async_copy(si_v.at[part], si_out.at[part], out_sem.at[c]).wait()
-    nb_store.wait()
-    drain(c1, xy_me, xy_group, c1s, c1r)
-    drain(c2, zc_me, zc_group, c2s, c2r)
+    drain(c1, zc_me, zc_group, c1s, c1r)
+    drain(c2, xy_me, xy_group, c2s, c2r)
     drain(e1, xy_me, xy_group, e1s, e1r)
-    ritz_out[...] = unpack(collect(e2, zc_me, zc_group, e2s, e2r))
+    energy = unpack(collect(e2, zc_me, zc_group, e2s, e2r))
+    ritz_out[...] = dot_nt(dot(inverse, energy, HIGHEST), inverse, HIGHEST)
     drain(e2, zc_me, zc_group, e2s, e2r)
+
+
+def hand_over(nb_v, ritz_v, si_v, nb_out, ritz_out, si_out, sems):
+    copies = [
+        pltpu.make_async_copy(src, dst, sems.at[i])
+        for i, (src, dst) in enumerate(((nb_v, nb_out), (si_v, si_out), (ritz_v, ritz_out)))
+    ]
+    for copy in copies:
+        copy.start()
+    for copy in copies:
+        copy.wait()
 
 
 def per_device(occupied, search_dirs, previous_dirs, occupied_image, previous_image, potential, ritz_vectors):
@@ -288,36 +331,48 @@
     vmem = pl.BlockSpec(memory_space=pltpu.VMEM)
     block = (ORB, LX, LY, LZ)
     dma = pltpu.SemaphoreType.DMA
+    results = pl.pallas_call(
+        kernel,
+        out_shape=(pltpu.VMEM(block, BF16), pltpu.VMEM((ORB, ORB), F32), pltpu.VMEM(block, BF16)),
+        in_specs=[pl.BlockSpec(memory_space=pltpu.HBM)] * 11,
+        out_specs=(vmem, vmem, vmem),
+        scratch_shapes=[pltpu.VMEM(block, BF16)] * 5
+        + [pltpu.VMEM((LX, LY, LZ), F32)]
+        + [pltpu.VMEM(block, BF16)] * 4
+        + [
+            pltpu.VMEM((ROWS, 3 * ROWS), BF16),
+            pltpu.VMEM((2 * ROWS, LX * LZ), BF16),
+            pltpu.VMEM((ORB, 5 * GR * LY), F32),
+            pltpu.VMEM((ROWS, ROWS), BF16),
+            pltpu.VMEM((ROWS, ROWS), BF16),
+            pltpu.VMEM((ORB, 3 * ORB), BF16),
+            pltpu.VMEM(amat.shape, BF16),
+            pltpu.VMEM(zmat.shape, BF16),
+            pltpu.VMEM(rep.shape, BF16),
+            pltpu.VMEM(rep96.shape, BF16),
+        ]
+        + [pltpu.VMEM((16, 8, 128), F32)] * 4
+        + [dma((11,)), dma((4, NCH)), dma((4, NCH))]
+        + [dma((16,))] * 8,
+        compiler_params=pltpu.CompilerParams(
+            collective_id=0, has_side_effects=True, vmem_limit_bytes=52 * 2**20
+        ),
+    )(
+        occupied, search_dirs, previous_dirs, occupied_image, previous_image, potential, ritz_vectors.T,
+        jnp.asarray(amat), jnp.asarray(zmat), jnp.asarray(rep), jnp.asarray(rep96),
+    )
     return pl.pallas_call(
-        kernel,
+        hand_over,
         out_shape=(
             jax.ShapeDtypeStruct(block, BF16),
             jax.ShapeDtypeStruct((ORB, ORB), F32),
             jax.ShapeDtypeStruct(block, BF16),
         ),
-        in_specs=[anywhere] * 6 + [vmem] * 5,
-        out_specs=(anywhere, vmem, anywhere),
-        scratch_shapes=[pltpu.VMEM(block, BF16)] * 5
-        + [pltpu.VMEM((LX, LY, LZ), F32)]
-        + [pltpu.VMEM(block, BF16)] * 6
-        + [
-            pltpu.VMEM((ROWS, 3 * ROWS), BF16),
-            pltpu.VMEM((2 * ROWS, LX * LZ), BF16),
-            pltpu.VMEM((ORB, 3 * ROWS), F32),
-            pltpu.VMEM((3 * ROWS, ORB), F32),
-            pltpu.VMEM((ROWS, ROWS), BF16),
-            pltpu.VMEM((ROWS, ROWS), BF16),
-        ]
-        + [pltpu.VMEM((16, 8, 128), F32)] * 4
-        + [dma((6,)), dma((4, NCH)), dma((4, NCH)), dma((NCH + 1,))]
-        + [dma((16,))] * 8,
-        compiler_params=pltpu.CompilerParams(
-            collective_id=0, has_side_effects=True, vmem_limit_bytes=56 * 2**20
-        ),
-    )(
-        occupied, search_dirs, previous_dirs, occupied_image, previous_image, potential, ritz_vectors,
-        jnp.asarray(amat), jnp.asarray(zmat), jnp.asarray(rep), jnp.asarray(rep96),
-    )
+        in_specs=[vmem, vmem, vmem],
+        out_specs=(anywhere, anywhere, anywhere),
+        scratch_shapes=[dma((3,))],
+        compiler_params=pltpu.CompilerParams(vmem_limit_bytes=2**20),
+    )(*[pltpu.with_memory_space_constraint(result, pltpu.VMEM) for result in results])
 
 
 def solution(mesh):

time: 73.7 us -> 53.2 us (0.72)
  Pallas kernels: 67.5 us -> 52.4 us
  local copies, waits for them, and re-layouts: 5.38 us -> 0 us
    pallas_call x1 -> x2, Pallas kernels: 67.5 us -> 52.4 us  [the longest x1 51 us: per_device(): pl.pallas_call(kernel, out_shape=(pltpu.VMEM(block, BF16), pltpu.VMEM((OR...]
    unnamed x8 -> x0, local copies, waits for them, and re-layouts: 5.38 us -> none
where the time goes in v2:
time: 53.2 us; the launch traced here: 53 us
  Pallas kernels  52.4 us (98%)
  between operations  0.64 us (1%)
    pallas_call x1, Pallas kernels, per_device(): pl.pallas_call(kernel, out_shape=(pltpu.VMEM(block, BF16), pltpu.VMEM((OR...  51 us
    pallas_call x1, Pallas kernels, per_device(): pl.pallas_call(hand_over, out_shape=(jax.ShapeDtypeStruct(block, BF16), j...  1.35 us

profile of v2, /device:TPU:1, one launch (start us, length us, event | category | flops | bytes accessed | tf_op | source)
XLA Modules:
  0.0 53.0 jit_solution(3533546031349322452)
XLA Ops:
  0.6 51.0 %shard_map.130 = (bf16[32,4,16,256]{3,2,1,0:T(8,128)(2,1)S(1)}, f32[32,32]{1,0:T(8,128)S(1)}, bf16[32,4,16,256]{3,2,1,0:T(8,128)(2,1)S(1)}) custom-call(bf16[32,4,16,256]{3,2,1,0:T(8,128)(2,1)} %occ.1, bf16[32,4,16,256]{3,2,1,0:T(8,128)(2,1)} %sea.1, bf16[32,4,16,256]{3,2,1,0:T(8,128)(2,1)} %pre.1, bf16[32,4,16,256]{3,2,1,0:T(8,128)(2,1)} %occ_im.1, ...), custom_call_target="tpu_custom_call" | custom-call | tf_op jit(solution)/shard_map/pallas_call | solution.py:334
  51.7 1.3 %shard_map.131 = (bf16[32,4,16,256]{3,2,1,0:T(8,128)(2,1)}, f32[32,32]{1,0:T(8,128)}, bf16[32,4,16,256]{3,2,1,0:T(8,128)(2,1)}) custom-call(bf16[32,4,16,256]{3,2,1,0:T(8,128)(2,1)S(1)} %get-tuple-element.6.nb_v, f32[32,32]{1,0:T(8,128)S(1)} %get-tuple-element.7.ritz_v, bf16[32,4,16,256]{3,2,1,0:T(8,128)(2,1)S(1)} %get-tuple-element.8.si_v), custom_call_target="tpu_custom_call" | custom-call | tf_op jit(solution)/shard_map/pallas_call | solution.py:364

commit v3 on v2

--- a/solution.py
+++ b/solution.py
@@ -17,7 +17,9 @@
 LX, LY, LZ = 4, 16, 256
 NGX, NGY = 32, 8
 NXC, NYC, NZC, NC = 4, 4, 8, 2
-SENT = (3, 6)
+SENT = 3
+PIECES = 1
+SLOTS = (NC, NZC, NYC, NXC, NXC * NYC, NZC * NC)
 EARLY = 1
 CH = 4
 NCH = ORB // CH
@@ -92,14 +94,15 @@
     [o for o in itertools.product(range(NZC), range(NC)) if o != (0, 0)],
     key=lambda o: -(ring_distance(o[0], NZC) + 0.5 * o[1]),
 )
+Z_OFFSETS = sorted(range(1, NZC), key=lambda d: -ring_distance(d, NZC))
 
 
 def kernel(
     occ, sea, pre, occ_im, pre_im, pot, ritz_in, amat_in, zmat_in, rep_in, rep96_in,
     nb_v, ritz_out, si_v,
     o_v, s_v, p_v, oi_v, pi_v, v_v, xl, xr, yl, yr, rk, rot, grams, kh, kl, ritz, amat, zmat, rep, rep96,
-    c1, c2, e1, e2,
-    load_sem, send_sem, recv_sem, c1s, c1r, c2s, c2r, e1s, e1r, e2s, e2r,
+    c0, c1, c2, c3, e1, e2,
+    load_sem, send_sem, recv_sem, c0s, c0r, c1s, c1r, c2s, c2r, c3s, c3r, e1s, e1r, e2s, e2r,
 ):
     gx, gy = lax.axis_index("gx"), lax.axis_index("gy")
     z, x, y, core = gx // NXC, lax.rem(gx, NXC), gy // NC, lax.rem(gy, NC)
@@ -121,14 +124,21 @@
     for dx, dy in XY_OFFSETS:
         px, py = lax.rem(x + dx, NXC), lax.rem(y + dy, NYC)
         xy_group.append((px * NYC + py, (z * NXC + px, py * NC + core)))
+    z_group = []
+    for dz in Z_OFFSETS:
+        pz = lax.rem(z + dz, NZC)
+        z_group.append((pz, (pz * NXC + x, gy)))
+    pair = [(1 - core, (gx, y * NC + 1 - core))]
     zc_group = []
     for dz, dc in ZC_OFFSETS:
         pz, pc = lax.rem(z + dz, NZC), lax.rem(core + dc, NC)
         zc_group.append((pz * NC + pc, (pz * NXC + x, y * NC + pc)))
     xy_me, zc_me = x * NYC + y, z * NC + core
+    x_group = [(lax.rem(x + d, NXC), (z * NXC + lax.rem(x + d, NXC), gy)) for d in (2, 1, 3)]
+    y_group = [(lax.rem(y + d, NYC), (gx, lax.rem(y + d, NYC) * NC + core)) for d in (2, 1, 3)]
 
     barrier = pltpu.get_barrier_semaphore()
-    others = neighbours + [d for _, d in xy_group] + [d for _, d in zc_group]
+    others = neighbours + [d for _, d in xy_group + zc_group]
     for device in others:
         pl.semaphore_signal(barrier, inc=1, device_id=device, device_id_type=MESH)
     pl.semaphore_wait(barrier, len(others))
@@ -150,7 +160,7 @@
     send_chunks(0, 1)
     for load in loads:
         load.start()
-    send_chunks(1, SENT[0])
+    send_chunks(1, SENT)
 
     def post(buf, me, group, sends, recvs, value):
         buf[me] = value
@@ -165,7 +175,7 @@
                 buf.at[slot], buf.at[slot], sends.at[i], recvs.at[slot], device_id=device, device_id_type=MESH
             ).wait_recv()
         total = buf[0]
-        for slot in range(1, 16):
+        for slot in range(1, buf.shape[0]):
             total = total + buf[slot]
         return total
 
@@ -216,11 +226,10 @@
     high_high = dot_split(folded[:, 0:ROWS], rep[...])
     high_low = dot_split(folded[:, ROWS : 2 * ROWS], rep[...])
     correlation = high_high + high_low + high_low.T
-    post(c1, zc_me, zc_group, c1s, c1r, pack(correlation))
-    send_chunks(SENT[0], SENT[1])
-
-    def gram(ref, first):
-        rows = jnp.concatenate([ref[first : first + GR, i].reshape(GR * LY, LZ) for i in range(LX)], axis=1)
+    post(c0, core, pair, c0s, c0r, pack(correlation))
+
+    def gram(ref, first, count=GR):
+        rows = jnp.concatenate([ref[first : first + count, i].reshape(count * LY, LZ) for i in range(LX)], axis=1)
         products = dot_nt(rot[...], rows)
         return masked(products[0:ROWS] + products[ROWS : 2 * ROWS]).sum(axis=1)
 
@@ -243,6 +252,8 @@
     loads[6].wait()
     grams[:, 0:256] = gram(oi_v, 0)
     grams[:, 256:512] = gram(oi_v, GR)
+    post(c1, z, z_group, c1s, c1r, collect(c0, core, pair, c0s, c0r))
+    send_chunks(SENT, NCH)
     loads[7].wait()
     grams[:, 768:1024] = gram(pi_v, 0)
     grams[:, 1024:1280] = gram(pi_v, GR)
@@ -251,8 +262,7 @@
     def _(c):
         stencil_chunk(c)
 
-    post(c2, xy_me, xy_group, c2s, c2r, collect(c1, zc_me, zc_group, c1s, c1r))
-    send_chunks(SENT[1], NCH)
+    post(c2, y, y_group, c2s, c2r, collect(c1, z, z_group, c1s, c1r))
 
     @pl.loop(EARLY, NCH // 2)
     def _(c):
@@ -261,14 +271,25 @@
     grams[:, 512:768] = gram(si_v, 0)
     early = dot_split(grams[:, 0:768], ritz_rows[0:768]) + dot_split(grams[:, 768:1280], ritz_rows[1024:1536])
 
-    @pl.loop(NCH // 2, NCH)
+    post(c3, x, x_group, c3s, c3r, collect(c2, y, y_group, c2s, c2r))
+
+    @pl.loop(NCH // 2, NCH - 1)
     def _(c):
         stencil_chunk(c)
 
-    energy = early + dot_split(gram(si_v, GR), ritz_rows[768:1024])
+    grams[:, 1280:1472] = gram(si_v, GR, GR - CH)
+    early = early + dot_split(grams[:, 1280:1472], ritz_rows[768:960])
+
+    @pl.loop(NCH - 1, NCH)
+    def _(c):
+        stencil_chunk(c)
+
+    energy = early + dot_split(gram(si_v, ORB - CH, CH), ritz_rows[960:1024])
     post(e1, xy_me, xy_group, e1s, e1r, pack(energy))
 
-    correlation = unpack(collect(c2, xy_me, xy_group, c2s, c2r))
+    post(e2, zc_me, zc_group, e2s, e2r, collect(e1, xy_me, xy_group, e1s, e1r))
+
+    correlation = unpack(collect(c3, x, x_group, c3s, c3r))
 
     lane = lax.broadcasted_iota(jnp.int32, (ORB, 2 * ORB), 1)
     row = lax.broadcasted_iota(jnp.int32, (ORB, 2 * ORB), 0)
@@ -289,8 +310,6 @@
         spread = dot(rep[...], dot_nt(part, rep[...]).astype(BF16))
         ref[...] = masked(spread).reshape(ROWS, ROWS).astype(BF16)
 
-    post(e2, zc_me, zc_group, e2s, e2r, collect(e1, xy_me, xy_group, e1s, e1r))
-
     def rotate(i):
         columns = pl.ds(pl.multiple_of(i * LZ, LZ), LZ)
         high, low = rot[0:ROWS, columns], rot[ROWS : 2 * ROWS, columns]
@@ -304,8 +323,10 @@
     for way in range(4):
         for c in range(NCH):
             halo_copy(way, c).wait_send()
-    drain(c1, zc_me, zc_group, c1s, c1r)
-    drain(c2, xy_me, xy_group, c2s, c2r)
+    drain(c0, core, pair, c0s, c0r)
+    drain(c1, z, z_group, c1s, c1r)
+    drain(c2, y, y_group, c2s, c2r)
+    drain(c3, x, x_group, c3s, c3r)
     drain(e1, xy_me, xy_group, e1s, e1r)
     energy = unpack(collect(e2, zc_me, zc_group, e2s, e2r))
     ritz_out[...] = dot_nt(dot(inverse, energy, HIGHEST), inverse, HIGHEST)
@@ -313,10 +334,11 @@
 
 
 def hand_over(nb_v, ritz_v, si_v, nb_out, ritz_out, si_out, sems):
-    copies = [
-        pltpu.make_async_copy(src, dst, sems.at[i])
-        for i, (src, dst) in enumerate(((nb_v, nb_out), (si_v, si_out), (ritz_v, ritz_out)))
-    ]
+    pairs = [(ritz_v, ritz_out)]
+    for first in range(0, ORB, ORB // PIECES):
+        part = pl.ds(first, ORB // PIECES)
+        pairs += [(nb_v.at[part], nb_out.at[part]), (si_v.at[part], si_out.at[part])]
+    copies = [pltpu.make_async_copy(src, dst, sems.at[i]) for i, (src, dst) in enumerate(pairs)]
     for copy in copies:
         copy.start()
     for copy in copies:
@@ -342,7 +364,7 @@
         + [
             pltpu.VMEM((ROWS, 3 * ROWS), BF16),
             pltpu.VMEM((2 * ROWS, LX * LZ), BF16),
-            pltpu.VMEM((ORB, 5 * GR * LY), F32),
+            pltpu.VMEM((ORB, 6 * GR * LY), F32),
             pltpu.VMEM((ROWS, ROWS), BF16),
             pltpu.VMEM((ROWS, ROWS), BF16),
             pltpu.VMEM((ORB, 3 * ORB), BF16),
@@ -351,9 +373,9 @@
             pltpu.VMEM(rep.shape, BF16),
             pltpu.VMEM(rep96.shape, BF16),
         ]
-        + [pltpu.VMEM((16, 8, 128), F32)] * 4
+        + [pltpu.VMEM((n, 8, 128), F32) for n in SLOTS]
         + [dma((11,)), dma((4, NCH)), dma((4, NCH))]
-        + [dma((16,))] * 8,
+        + [dma((n,)) for n in SLOTS for _ in range(2)],
         compiler_params=pltpu.CompilerParams(
             collective_id=0, has_side_effects=True, vmem_limit_bytes=52 * 2**20
         ),
@@ -370,7 +392,7 @@
         ),
         in_specs=[vmem, vmem, vmem],
         out_specs=(anywhere, anywhere, anywhere),
-        scratch_shapes=[dma((3,))],
+        scratch_shapes=[dma((1 + 2 * PIECES,))],
         compiler_params=pltpu.CompilerParams(vmem_limit_bytes=2**20),
     )(*[pltpu.with_memory_space_constraint(result, pltpu.VMEM) for result in results])
 

time: 53.2 us -> 52.2 us (0.981)
  Pallas kernels: 52.4 us -> 51.4 us
    pallas_call x1, Pallas kernels: 51 us -> 50.1 us  [per_device(): pl.pallas_call(kernel, out_shape=(pltpu.VMEM(block, BF16), pltpu.VMEM((OR...]
where the time goes in v3:
time: 52.2 us; the launch traced here: 52.1 us
  Pallas kernels  51.4 us (98%)
  between operations  0.64 us (1%)
    pallas_call x1, Pallas kernels, per_device(): pl.pallas_call(kernel, out_shape=(pltpu.VMEM(block, BF16), pltpu.VMEM((OR...  50.1 us
    pallas_call x1, Pallas kernels, per_device(): pl.pallas_call(hand_over, out_shape=(jax.ShapeDtypeStruct(block, BF16), j...  1.35 us

profile of v3, /device:TPU:1, one launch (start us, length us, event | category | flops | bytes accessed | tf_op | source)
XLA Modules:
  0.0 52.1 jit_solution(191662783255901688)
XLA Ops:
  0.6 50.1 %shard_map.130 = (bf16[32,4,16,256]{3,2,1,0:T(8,128)(2,1)S(1)}, f32[32,32]{1,0:T(8,128)S(1)}, bf16[32,4,16,256]{3,2,1,0:T(8,128)(2,1)S(1)}) custom-call(bf16[32,4,16,256]{3,2,1,0:T(8,128)(2,1)} %occ.1, bf16[32,4,16,256]{3,2,1,0:T(8,128)(2,1)} %sea.1, bf16[32,4,16,256]{3,2,1,0:T(8,128)(2,1)} %pre.1, bf16[32,4,16,256]{3,2,1,0:T(8,128)(2,1)} %occ_im.1, ...), custom_call_target="tpu_custom_call" | custom-call | tf_op jit(solution)/shard_map/pallas_call | solution.py:356
  50.7 1.3 %shard_map.131 = (bf16[32,4,16,256]{3,2,1,0:T(8,128)(2,1)}, f32[32,32]{1,0:T(8,128)}, bf16[32,4,16,256]{3,2,1,0:T(8,128)(2,1)}) custom-call(bf16[32,4,16,256]{3,2,1,0:T(8,128)(2,1)S(1)} %get-tuple-element.6.nb_v, f32[32,32]{1,0:T(8,128)S(1)} %get-tuple-element.7.ritz_v, bf16[32,4,16,256]{3,2,1,0:T(8,128)(2,1)S(1)} %get-tuple-element.8.si_v), custom_call_target="tpu_custom_call" | custom-call | tf_op jit(solution)/shard_map/pallas_call | solution.py:386
